TPU v7x, 512 devices: a whole 4x4x16 slice. The times are simulated.
512 devices in a mesh: mem: 16 (over y, z_hi), tt: 32 (over x, z_lo, core).
Axes of the slice: x: 4, y: 4, z: 16 (z_hi: 4, z_lo: 4; z = z_hi * 4 + z_lo), core: 2. Of those that a mesh axis runs over, the one named last changes fastest.
Arguments:
- history: bfloat16 [2, 64, 128, 64, 128], P(None, 'mem', None, 'tt'), may hold values from -0.0625 to 0.0625
- free_rows: bfloat16 [2, 2, 128, 64, 128], P(None, None, None, 'tt'), may hold values from -3 to 3
- memory_start: int32 [2], replicated, may hold values from 0 to 31, as said below
- now: int32 [1], replicated, may hold values from 32 to 62
Outputs:
- new_rows: bfloat16 [2, 2, 128, 64, 128], P(None, None, None, 'tt')
Inputs may be any that keep to these rules, and one draw needn't show every extreme that they name: Row r's memory integral starts at memory_start[r]; starts need not be distinct, and some row starts at the largest allowed value. The new rows' times now + r lie inside the grid.
All inputs are finite; a program needn't handle non-finite values.
Results may differ from a plain program's by a relative error of at most 0.012.
The roundings to bfloat16 on the way count: a program that leaves them out, or rounds other values in their place, can miss the bound.
Values may be sent and summed in bfloat16 or wider, within the bound.
A program may use at most 64 MiB of HBM per device.

v0:
```python
import jax
import jax.numpy as jnp
from jax import lax
from jax.sharding import PartitionSpec as P

ITERS = 3


COUPLING = 0.5


def from_root(value, axis, source):
    kept = jnp.where(lax.axis_index(axis) == source, value, 0).astype(value.dtype)
    return lax.psum(kept, axis)


def self_energy(columns, live_weight):
    real_part = columns[0].astype(jnp.float32)
    imag_part = columns[1].astype(jnp.float32)
    modulus = real_part * real_part + imag_part * imag_part
    sig_real = (-(real_part * modulus) * live_weight).astype(jnp.bfloat16)
    sig_imag = (-(imag_part * modulus) * live_weight).astype(jnp.bfloat16)
    return (sig_real, sig_imag)


def memory_integral(sig_real, sig_imag, hist_real, hist_imag):
    out_real = jnp.dot(sig_real, hist_real, preferred_element_type=jnp.float32) - jnp.dot(
        sig_imag, hist_imag, preferred_element_type=jnp.float32
    )
    out_imag = jnp.dot(sig_real, hist_imag, preferred_element_type=jnp.float32) + jnp.dot(
        sig_imag, hist_real, preferred_element_type=jnp.float32
    )
    return jnp.stack([out_real, out_imag])


def on_device(history, free_rows, memory_start, now):
    tiles_per_mem = lax.axis_size("tt") // lax.axis_size("mem")
    row_count = free_rows.shape[1]
    orb_count = free_rows.shape[2]
    col_count = free_rows.shape[3]
    span_count = history.shape[1]
    hist_real = history[0].reshape(span_count * orb_count, col_count * orb_count)
    hist_imag = history[1].reshape(span_count * orb_count, col_count * orb_count)
    mem_index = lax.axis_index("mem")
    mem_times = mem_index * span_count + jnp.arange(span_count, dtype=jnp.int32)
    row_time = now[0] + jnp.arange(row_count, dtype=jnp.int32)
    live_mask = (mem_times[None, :] >= memory_start[:, None]) & (
        mem_times[None, :] < row_time[:, None]
    )
    live_weight = live_mask.astype(jnp.float32)[:, None, :, None]
    free_flat = free_rows.astype(jnp.float32).reshape(
        2, row_count * orb_count, col_count * orb_count
    )
    current = free_rows
    for sweep in range(ITERS):
        pieces = []
        for source in range(tiles_per_mem):
            pieces.append(from_root(current, "tt", mem_index * tiles_per_mem + source))
        columns = jnp.concatenate(pieces, axis=3)
        sig_real, sig_imag = self_energy(columns, live_weight)
        flat_real = sig_real.reshape(row_count * orb_count, span_count * orb_count)
        flat_imag = sig_imag.reshape(row_count * orb_count, span_count * orb_count)
        partial_value = memory_integral(flat_real, flat_imag, hist_real, hist_imag)
        summed = lax.psum(partial_value, "mem")
        current = (free_flat + COUPLING * summed).astype(jnp.bfloat16).reshape(free_rows.shape)
    return current


def solution(mesh):
    return jax.shard_map(
        on_device,
        mesh=mesh,
        in_specs=(P(None, "mem", None, "tt", None), P(None, None, None, "tt", None), P(), P()),
        out_specs=P(None, None, None, "tt", None),
        check_vma=False,
    )
```

profile of v0, /device:TPU:1, one launch (start us, length us, event | category | flops | bytes accessed | tf_op | source)
XLA Modules:
  0.0 1499.2 jit_solution(73152920087149187)
XLA Ops:
  6.5 2.2 broadcast_select_fusion.1
  9.5 0.6 copy-done.2
  10.2 0.4 fusion.90
  10.6 291.7 %all-reduce.20.cloned.1.call-done = (bf16[2,2,128,2,128]{4,3,2,1,0:T(2,128)(2,1)}, bf16[2,2,128,2,128]{4,3,2,1,0:T(2,128)(2,1)}) async-done(((bf16[2,2,128,2,128]{4,3,2,1,0:T(2,128)(2,1)}, bf16[2,2,128,2,128]{4,3,2,1,0:T(2,128)(2,1)}), (bf16[2,2,128,2,128]{4,3,2,1,0:T(2,128)(2,1)}, bf16[2,2,128,2,128]{4,3,2,1,0:T(2,128)(2,1)})) %all-reduce.20.cloned.1.call-update) | async-done | bytes 524304 | tf_op jit(solution)/shard_map/psum | solution.py:14
  302.2 2.4 fusion.12
  305.6 0.8 pad_maximum_fusion
  306.5 0.9 copy-done
  307.5 194.7 %all-reduce.10.cloned.1.call-done = f32[2,256,256]{2,1,0:T(8,128)} async-done(((f32[2,256,256]{2,1,0:T(8,128)}), f32[2,256,256]{2,1,0:T(8,128)}) %all-reduce.10.cloned.1.call-update) | async-done | bytes 524304 | tf_op jit(solution)/shard_map/psum | solution.py:64
  502.2 1.1 broadcast_select_fusion.5
  503.3 0.8 select_n.52
  504.1 0.8 select_n.55
  504.9 291.3 %all-reduce.18.cloned.1.call-done = (bf16[2,2,128,2,128]{4,3,2,1,0:T(2,128)(2,1)}, bf16[2,2,128,2,128]{4,3,2,1,0:T(2,128)(2,1)}) async-done(((bf16[2,2,128,2,128]{4,3,2,1,0:T(2,128)(2,1)}, bf16[2,2,128,2,128]{4,3,2,1,0:T(2,128)(2,1)}), (bf16[2,2,128,2,128]{4,3,2,1,0:T(2,128)(2,1)}, bf16[2,2,128,2,128]{4,3,2,1,0:T(2,128)(2,1)})) %all-reduce.18.cloned.1.call-update) | async-done | bytes 524304 | tf_op jit(solution)/shard_map/psum | solution.py:14
  796.3 2.4 fusion.19
  799.6 0.8 pad_maximum_fusion.1
  800.5 195.9 %all-reduce.12.cloned.1.call-done = f32[2,256,256]{2,1,0:T(8,128)} async-done(((f32[2,256,256]{2,1,0:T(8,128)}), f32[2,256,256]{2,1,0:T(8,128)}) %all-reduce.12.cloned.1.call-update) | async-done | bytes 524304 | tf_op jit(solution)/shard_map/psum | solution.py:64
  996.4 1.1 broadcast_select_fusion.4
  997.6 0.8 select_n.57
  998.4 0.8 select_n.59
  999.2 291.3 %all-reduce.16.cloned.1.call-done = (bf16[2,2,128,2,128]{4,3,2,1,0:T(2,128)(2,1)}, bf16[2,2,128,2,128]{4,3,2,1,0:T(2,128)(2,1)}) async-done(((bf16[2,2,128,2,128]{4,3,2,1,0:T(2,128)(2,1)}, bf16[2,2,128,2,128]{4,3,2,1,0:T(2,128)(2,1)}), (bf16[2,2,128,2,128]{4,3,2,1,0:T(2,128)(2,1)}, bf16[2,2,128,2,128]{4,3,2,1,0:T(2,128)(2,1)})) %all-reduce.16.cloned.1.call-update) | async-done | bytes 524304 | tf_op jit(solution)/shard_map/psum | solution.py:14
  1290.5 2.4 fusion.26
  1293.8 0.8 pad_maximum_fusion.2
  1294.6 195.8 %all-reduce.14.cloned.1.call-done = f32[2,256,256]{2,1,0:T(8,128)} async-done(((f32[2,256,256]{2,1,0:T(8,128)}), f32[2,256,256]{2,1,0:T(8,128)}) %all-reduce.14.cloned.1.call-update) | async-done | bytes 524304 | tf_op jit(solution)/shard_map/psum | solution.py:64
  1490.4 1.1 add_convert_fusion
  1491.5 0.8 reshape.321
  (34 shorter events, 3.4 us)
Async XLA Ops:
  6.5 295.7 %all-reduce.20.cloned.1.call-start = ((), (), s32[]{:S(2)}) async-start(), calls=%async_computation.5 | async-start | bytes 1048576 | tf_op jit(solution)/shard_map/psum | solution.py:14
  6.5 3.7 copy-start.1
  8.8 493.4 %all-reduce.10.cloned.1.call-start = ((), (), s32[]{:S(2)}) async-start(), calls=%async_computation | async-start | bytes 1048576 | tf_op jit(solution)/shard_map/psum | solution.py:64
  9.5 0.7 copy-start.2
  306.4 0.9 copy-start
  306.4 489.9 %all-reduce.18.cloned.1.call-start = ((), (), s32[]{:S(2)}) async-start(), calls=%async_computation.4 | async-start | bytes 1048576 | tf_op jit(solution)/shard_map/psum | solution.py:14
  504.9 491.5 %all-reduce.12.cloned.1.call-start = ((), (), s32[]{:S(2)}) async-start(), calls=%async_computation.1 | async-start | bytes 1048576 | tf_op jit(solution)/shard_map/psum | solution.py:64
  800.5 490.0 %all-reduce.16.cloned.1.call-start = ((), (), s32[]{:S(2)}) async-start(), calls=%async_computation.3 | async-start | bytes 1048576 | tf_op jit(solution)/shard_map/psum | solution.py:14
  999.2 491.3 %all-reduce.14.cloned.1.call-start = ((), (), s32[]{:S(2)}) async-start(), calls=%async_computation.2 | async-start | bytes 1048576 | tf_op jit(solution)/shard_map/psum | solution.py:64
Sparse Core Ops, SparseCore 0:
  10.3 291.8 all-reduce.19
  306.5 195.6 all-reduce.9
  505.1 291.1 all-reduce.17
  800.6 195.8 all-reduce.11
  999.3 291.1 all-reduce.15
  1294.8 195.6 all-reduce.13
where the time goes:
time: 1510 us; the launch traced here: 1500 us
  waiting for transfers between devices  1460 us (97%)
  other arithmetic  15.3 us (1%)
    psum x3, waiting for transfers between devices, from_root(): return lax.psum(kept, axis)  874 us
    psum x3, waiting for transfers between devices, on_device(): summed = lax.psum(partial_value, 'mem')  586 us
  transfers between devices with their start and end apart: 6, of which 6 were waited for; matrix products, arithmetic and copies ran while one was open for 0% of the time, Pallas kernels for 0%

commit v1 on v0

v1 whole, which is shorter than its diff:
```python
import functools

import jax
import jax.numpy as jnp
from jax import lax
from jax.experimental import pallas as pl
from jax.experimental.pallas import tpu as pltpu
from jax.sharding import PartitionSpec as P

ITERS = 3
COUPLING = 0.5
MESH = pl.DeviceIdType.MESH
BF16 = jnp.bfloat16
F32 = jnp.float32


def device(x, y, zh, zl, c):
    return (y * 4 + zh, x * 8 + zl * 2 + c)


def kernel(
    hist, free, start, now, out,
    hraw, htmp, h_all, fraw, ftmp, fpc, fa, fb, gsend, grecv, rsend, rrecv, xfin, pieces, otmp,
    lsem, hy_s, hy_r, hs_s, hs_r, f_s, f_r, g_s, g_r, r_s, r_r, az_s, az_r, ay_s, ay_r,
):
    mem, tt = lax.axis_index("mem"), lax.axis_index("tt")
    y, zh = mem // 4, mem % 4
    x, zl, c = tt // 8, (tt // 2) % 4, tt % 2
    sib = device(x, y, zh, zl, 1 - c)

    def remote(src, dst, ssem, rsem, dev):
        return pltpu.make_async_remote_copy(
            src_ref=src, dst_ref=dst, send_sem=ssem, recv_sem=rsem, device_id=dev, device_id_type=MESH
        )

    load_h = pltpu.make_async_copy(hist, hraw, lsem.at[0])
    load_f = pltpu.make_async_copy(free, fraw, lsem.at[1])
    load_h.start()
    load_f.start()

    barrier = pltpu.get_barrier_semaphore()
    partners = []
    for dz in range(16):
        z = (zh * 4 + zl + dz) % 16
        for dc in range(2):
            if dz or dc:
                partners.append(device(x, y, z // 4, z % 4, (c + dc) % 2))
    for dx in range(1, 4):
        for dz in range(4):
            partners.append(device((x + dx) % 4, y, zh, (zl + dz) % 4, c))
    for dy in range(1, 4):
        partners.append(device(x, (y + dy) % 4, zh, zl, c))
    for dev in partners:
        pl.semaphore_signal(barrier, inc=1, device_id=dev, device_id_type=MESH)

    load_f.wait()
    for part in range(2):
        for r in range(2):
            rows = pl.ds(pl.multiple_of(y * 64, 64), 64)
            ftmp[part, r] = fraw[part, r, rows, :].astype(F32)
    for part in range(2):
        for r in range(2):
            for t in range(2):
                fpc[t, r, part * 32 : part * 32 + 32, :] = ftmp[part, r, pl.ds(t, 32, stride=2), :].astype(BF16)

    load_h.wait()
    for sl in range(4):
        for part in range(2):
            htmp[sl, part] = hraw[part, sl].astype(F32)
        for part in range(2):
            for t in range(2):
                col = (t * 2 + part) * 128
                h_all[y, c, sl * 128 : sl * 128 + 128, col : col + 128] = htmp[
                    sl, part, pl.ds(t, 128, stride=2), :
                ].astype(BF16)

    pl.semaphore_wait(barrier, len(partners))
    sends = []

    for t in range(2):
        for r in range(2):
            to = 2 * c + t
            mine = (zl == to) & (c == r)

            @pl.when((zl == zh) & mine)
            def _():
                fa[...] = fpc[t, r]

            @pl.when((zl == zh) & jnp.logical_not(mine))
            def _():
                remote(fpc.at[t, r], fa, f_s.at[t * 2 + r], f_r.at[0], device(x, y, zh, to, r)).start()

    @pl.when(c == zh // 2)
    def _():
        fb[...] = fpc[zh % 2, c]
        remote(fpc.at[zh % 2, 1 - c], fb, f_s.at[4], f_r.at[1], sib).start()

    up, down, far = (y + 1) % 4, (y + 3) % 4, (y + 2) % 4
    up_dev, down_dev = device(x, up, zh, zl, c), device(x, down, zh, zl, c)

    def slab(b, core, sl):
        return h_all.at[b, core, pl.ds(sl * 128, 128), :]

    def hy(b, sl, k, dev):
        cp = remote(slab(b, c, sl), slab(b, c, sl), hy_s.at[k], hy_r.at[k], dev)
        cp.start()
        sends.append(cp)

    def hs(b, sl, k):
        cp = remote(slab(b, c, sl), slab(b, c, sl), hs_s.at[k], hs_r.at[k], sib)
        cp.start()
        sends.append(cp)

    def hy_wait(b, sl, k):
        remote(slab(b, c, sl), slab(b, c, sl), hy_s.at[k], hy_r.at[k], up_dev).wait_recv()

    for k in range(4):
        hy(y, k, k, up_dev)
        hy(y, (k + 2) % 4, 4 + k, down_dev)
    for k in range(4):
        hs(y, k, k)

    @pl.when(jnp.logical_not((zl == zh) & (c == zl // 2)))
    def _():
        remote(fpc.at[0, 0], fa, f_s.at[0], f_r.at[0], sib).wait_recv()

    s_time = 16 * x + 4 * zh + zl
    live = jnp.where((start[c] <= s_time) & (s_time < now[0] + c), 1.0, 0.0).astype(F32)

    def gather(n, value):
        re, im = value[:32].astype(F32), value[32:].astype(F32)
        mod = re * re + im * im
        gsend[n, :32, :] = (-(re * mod) * live).astype(BF16)
        gsend[n, 32:, :] = (-(im * mod) * live).astype(BF16)
        for dx, dz in G_ORDER:
            dev = device((x + dx) % 4, y, zh, (zl + dz) % 4, c)
            cp = remote(gsend.at[n], grecv.at[n, x, zl], g_s.at[n, dx * 4 + dz], g_r.at[n, x, zl], dev)
            cp.start()
            sends.append(cp)
        grecv[n, x, zl] = gsend[n]

    def g_wait(n, dx):
        for dz in range(4):
            if dx or dz:
                b = grecv.at[n, (x + dx) % 4, (zl + dz) % 4]
                remote(b, b, g_s.at[n, 0], g_r.at[n, (x + dx) % 4, (zl + dz) % 4], sib).wait_recv()

    def multiply(n, order, wait):
        acc = [None, None]
        for d in order:
            if wait:
                g_wait(n, d)
            b = (x + d) % 4 if wait else (y + d) % 4
            left = jnp.concatenate([grecv[n, b, sl] for sl in range(4)], axis=1)
            for core in range(2):
                prod = jnp.dot(left, h_all[b, core], preferred_element_type=F32)
                acc[core] = prod if acc[core] is None else acc[core] + prod
        for t in range(4):
            p = acc[t // 2][:, (t % 2) * 256 : (t % 2) * 256 + 256]
            rsend[n, t, :32, :] = (p[:32, :128] - p[32:, 128:]).astype(BF16)
            rsend[n, t, 32:, :] = (p[:32, 128:] + p[32:, :128]).astype(BF16)

    def r_send(n, last):
        for t in range(4):
            if last:
                here, dev = zh == t, device(x, y, t, zl, c)
            else:
                here, dev = (zh == zl) & (zl == t), device(x, y, zl, t, c)

            @pl.when(here)
            def _():
                rrecv[n, zh] = rsend[n, t]

            @pl.when(jnp.logical_not(here))
            def _():
                remote(rsend.at[n, t], rrecv.at[n, zh], r_s.at[n, t], r_r.at[n, zh], dev).start()

    def r_each(n, last, do):
        for t in range(4):
            here = (zh == t) if last else (zh == zl) & (zl == t)
            pl.when(jnp.logical_not(here))(functools.partial(do, t))

    def r_sum(n, last, base):
        for src in range(4):
            here = (zh == src) if last else (zh == zl) & (zh == src)

            @pl.when(jnp.logical_not(here))
            def _():
                remote(rrecv.at[n, src], rrecv.at[n, src], r_s.at[n, src], r_r.at[n, src], sib).wait_recv()

        total = rrecv[n, 0].astype(F32) + rrecv[n, 1].astype(F32) + rrecv[n, 2].astype(F32) + rrecv[n, 3].astype(F32)
        return (base[...].astype(F32) + COUPLING * total).astype(BF16)

    gather(0, fa[...])

    for k in range(4):
        hy_wait(down, k, k)
        if k < 2:
            hy(down, k, 8 + k, up_dev)
        hs(down, k, 4 + k)
        sl = (k + 2) % 4
        hy_wait(up, sl, 4 + k)
        if k < 2:
            hy(up, sl, 10 + k, down_dev)
        hs(up, sl, 8 + k)
    for k in range(2):
        hy_wait(far, k, 8 + k)
        hs(far, k, 12 + k)
        hy_wait(far, k + 2, 10 + k)
        hs(far, k + 2, 14 + k)
    for d in range(4):
        g_wait(0, d)
    for b, ks in ((y, ((0, 0), (1, 1), (2, 2), (3, 3))), (down, ((0, 4), (1, 5), (2, 6), (3, 7))),
                  (up, ((2, 8), (3, 9), (0, 10), (1, 11))), (far, ((0, 12), (1, 13), (2, 14), (3, 15)))):
        for sl, k in ks:
            remote(slab(b, 1 - c, sl), slab(b, 1 - c, sl), hs_s.at[k], hs_r.at[k], sib).wait_recv()

    for n in range(ITERS):
        last = n == ITERS - 1
        multiply(n, (0, 1, 3, 2), n > 0)
        r_send(n, last)
        if not last:
            gather(n + 1, r_sum(n, last, fa))

    @pl.when(c != zh // 2)
    def _():
        remote(fpc.at[0, 0], fb, f_s.at[4], f_r.at[1], sib).wait_recv()

    xfin[...] = r_sum(ITERS - 1, True, fb)

    core = zh // 2
    for d in (2, 1, 3, 0):
        dev = device(x, y, (zh + d) % 4, zl, core)

        def go(d=d, dev=dev):
            remote(xfin, pieces.at[y, zh % 2, c], az_s.at[d], az_r.at[zh % 2, c], dev).start()

        if d:
            go()
        else:
            @pl.when(core != c)
            def _():
                go()

            @pl.when(core == c)
            def _():
                pieces[y, zh % 2, c] = xfin[...]

    near = jnp.where((zh == 2 * c) | (zh == (2 * c + 3) % 4), 0, 1)
    for order in range(2):
        t = near if order == 0 else 1 - near
        for r in range(2):
            src = pieces.at[y, t, r]

            @pl.when(jnp.logical_not((zh == 2 * c + t) & (c == r)))
            def _():
                remote(src, src, az_s.at[0], az_r.at[t, r], sib).wait_recv()

            for dy in (2, 1, 3):
                k = (dy - 1) * 4 + order * 2 + r
                cp = remote(src, src, ay_s.at[k], ay_r.at[y, t, r], device(x, (y + dy) % 4, zh, zl, c))
                cp.start()
                sends.append(cp)

    def assemble(b):
        for t in range(2):
            for r in range(2):
                for part in range(2):
                    otmp[part, r, pl.ds(pl.multiple_of(b * 64, 64) + t, 32, stride=2), :] = pieces[
                        b, t, r, part * 32 : part * 32 + 32, :
                    ].astype(F32)
        for r in range(2):
            for part in range(2):
                rows = pl.ds(pl.multiple_of(b * 64, 64), 64)
                out[part, r, rows, :] = otmp[part, r, rows, :].astype(BF16)

    assemble(y)
    for dy in (1, 3, 2):
        b = (y + dy) % 4
        for t in range(2):
            for r in range(2):
                remote(pieces.at[b, t, r], pieces.at[b, t, r], ay_s.at[0], ay_r.at[b, t, r], sib).wait_recv()
        assemble(b)

    for t in range(2):
        for r in range(2):
            @pl.when((zl == zh) & jnp.logical_not((zl == 2 * c + t) & (c == r)))
            def _():
                remote(fpc.at[t, r], fa, f_s.at[t * 2 + r], f_r.at[0], sib).wait_send()

    @pl.when(c == zh // 2)
    def _():
        remote(fpc.at[0, 0], fb, f_s.at[4], f_r.at[1], sib).wait_send()

    for n in range(ITERS):
        r_each(n, n == ITERS - 1, lambda t, n=n: remote(
            rsend.at[n, t], rrecv.at[n, t], r_s.at[n, t], r_r.at[n, t], sib).wait_send())
    for d in range(4):
        def done(d=d):
            remote(xfin, pieces.at[0, 0, 0], az_s.at[d], az_r.at[0, 0], sib).wait_send()

        if d:
            done()
        else:
            pl.when(core != c)(done)
    for cp in sends:
        cp.wait_send()


G_ORDER = tuple(
    sorted(
        ((dx, dz) for dx in range(4) for dz in range(4) if dx or dz),
        key=lambda d: -(min(d[0], 4 - d[0]) + min(d[1], 4 - d[1])),
    )
)


def on_device(history, free_rows, memory_start, now):
    vmem = pltpu.VMEM
    dma = pltpu.SemaphoreType.DMA
    result = pl.pallas_call(
        kernel,
        out_shape=jax.ShapeDtypeStruct((2, 2, 256, 128), BF16),
        in_specs=[
            pl.BlockSpec(memory_space=pl.ANY),
            pl.BlockSpec(memory_space=pl.ANY),
            pl.BlockSpec(memory_space=pltpu.SMEM),
            pl.BlockSpec(memory_space=pltpu.SMEM),
        ],
        out_specs=pl.BlockSpec(memory_space=pltpu.VMEM),
        scratch_shapes=[
            vmem((2, 4, 256, 128), BF16),
            vmem((4, 2, 256, 128), F32),
            vmem((4, 2, 512, 512), BF16),
            vmem((2, 2, 256, 128), BF16),
            vmem((2, 2, 64, 128), F32),
            vmem((2, 2, 64, 128), BF16),
            vmem((64, 128), BF16),
            vmem((64, 128), BF16),
            vmem((ITERS, 64, 128), BF16),
            vmem((ITERS, 4, 4, 64, 128), BF16),
            vmem((ITERS, 4, 64, 128), BF16),
            vmem((ITERS, 4, 64, 128), BF16),
            vmem((64, 128), BF16),
            vmem((4, 2, 2, 64, 128), BF16),
            vmem((2, 2, 256, 128), F32),
            dma((2,)),
            dma((12,)), dma((12,)),
            dma((16,)), dma((16,)),
            dma((5,)), dma((2,)),
            dma((ITERS, 16)), dma((ITERS, 4, 4)),
            dma((ITERS, 4)), dma((ITERS, 4)),
            dma((4,)), dma((2, 2)),
            dma((12,)), dma((4, 2, 2)),
        ],
        compiler_params=pltpu.CompilerParams(
            collective_id=0, has_side_effects=True, vmem_limit_bytes=48 * 1024 * 1024
        ),
        name="fixed_point",
    )(history.reshape(2, 4, 256, 128), free_rows.reshape(2, 2, 256, 128), memory_start, now)
    return result.reshape(free_rows.shape)


def solution(mesh):
    return jax.shard_map(
        on_device,
        mesh=mesh,
        in_specs=(P(None, "mem", None, "tt", None), P(None, None, None, "tt", None), P(), P()),
        out_specs=P(None, None, None, "tt", None),
        check_vma=False,
    )
```

time: 1510 us -> 95 us (0.06)
  waiting for transfers between devices: 1460 us -> 0 us
  Pallas kernels: 0 us -> 90.7 us
  other arithmetic: 15.3 us -> 0 us
    psum x6 -> x0, waiting for transfers between devices: 1460 us -> none  [the longest x3 874 us: from_root(): return lax.psum(kept, axis)]
    pallas_call x0 -> x1, Pallas kernels: none -> 90.7 us  [on_device(): pl.pallas_call(kernel, out_shape=jax.ShapeDtypeStruct((2, 2, 256, 128), B...]
  transfers between devices with their start and end apart: 6 -> 0, of which waited for: 6 -> 0; matrix products, arithmetic and copies ran while one was open for 0% -> 0% of each run, Pallas kernels for 0% -> 0%
where the time goes in v1:
time: 95 us; the launch traced here: 94.7 us
  Pallas kernels  90.7 us (95%)
  local copies, waits for them, and re-layouts  3.34 us (4%)
    pallas_call x1, Pallas kernels, on_device(): pl.pallas_call(kernel, out_shape=jax.ShapeDtypeStruct((2, 2, 256, 128), B...  90.7 us
    unnamed x7, local copies, waits for them, and re-layouts  3.34 us

profile of v1, /device:TPU:1, one launch (start us, length us, event | category | flops | bytes accessed | tf_op | source)
XLA Modules:
  0.0 94.7 jit_solution(4381028628350456256)
XLA Ops:
  0.7 0.0 copy-start.2
  0.7 0.6 copy-done.2
  1.3 0.0 copy-start
  1.3 1.0 %copy-done = bf16[2,4,128,2,128]{4,3,2,1,0:T(2,128)(2,1)S(1)} copy-done((bf16[2,4,128,2,128]{4,3,2,1,0:T(2,128)(2,1)S(1)}, bf16[2,4,128,2,128]{4,3,2,1,0:T(2,128)(2,1)}, u32[]{:S(2)}) %copy-start) | copy-done | bytes 524312
  2.4 0.0 copy-start.1
  2.4 0.9 %copy-done.1 = bf16[2,2,128,2,128]{4,3,2,1,0:T(2,128)(2,1)S(1)} copy-done((bf16[2,2,128,2,128]{4,3,2,1,0:T(2,128)(2,1)S(1)}, bf16[2,2,128,2,128]{4,3,2,1,0:T(2,128)(2,1)}, u32[]{:S(2)}) %copy-start.1) | copy-done | bytes 262168
  3.3 90.7 %fixed_point.1 = bf16[2,2,256,128]{3,2,1,0:T(8,128)(2,1)S(1)} custom-call(bf16[2,4,256,128]{3,2,1,0:T(8,128)(2,1)S(1)} %bitcast.4, bf16[2,2,256,128]{3,2,1,0:T(8,128)(2,1)S(1)} %bitcast.5, s32[2]{0:T(128)S(1)} %copy-done.2, s32[1]{0:T(128)S(6)} %copy.6.now), custom_call_target="tpu_custom_call" | custom-call | tf_op jit(solution)/shard_map/fixed_point/pallas_call | solution.py:321
  94.0 0.7 copy.7
Async XLA Ops:
  0.7 0.7 copy-start.2
  1.3 1.0 %copy-start = (bf16[2,4,128,2,128]{4,3,2,1,0:T(2,128)(2,1)S(1)}, bf16[2,4,128,2,128]{4,3,2,1,0:T(2,128)(2,1)}, u32[]{:S(2)}) copy-start(bf16[2,4,128,2,128]{4,3,2,1,0:T(2,128)(2,1)} %param.4) | copy-start | bytes 1572868
  2.4 0.9 %copy-start.1 = (bf16[2,2,128,2,128]{4,3,2,1,0:T(2,128)(2,1)S(1)}, bf16[2,2,128,2,128]{4,3,2,1,0:T(2,128)(2,1)}, u32[]{:S(2)}) copy-start(bf16[2,2,128,2,128]{4,3,2,1,0:T(2,128)(2,1)} %param.5) | copy-start | bytes 786436

commit v2 on v1

v2 whole, which is shorter than its diff:
```python
import functools

import jax
import jax.numpy as jnp
from jax import lax
from jax.experimental import pallas as pl
from jax.experimental.pallas import tpu as pltpu
from jax.sharding import PartitionSpec as P

ITERS = 3
COUPLING = 0.5
MESH = pl.DeviceIdType.MESH
BF16 = jnp.bfloat16
F32 = jnp.float32
CHUNKS = 2
VMEM_KIB = 54784
ROWS = 32 // CHUNKS


def device(x, y, zh, zl, c):
    return (y * 4 + zh, x * 8 + zl * 2 + c)


def kernel(
    hist, free, start, now, out,
    start_s, now_s, hraw, htmp, h_all, fraw, ftmp, fpc, fa, fb, gsend, grecv, rsend, rrecv, xfin, pieces, otmp,
    lsem, hy_s, hy_r, hs_s, hs_r, f_s, f_r, g_s, g_r, r_s, r_r, az_s, az_r, ay_s, ay_r, known,
):
    mem, tt = lax.axis_index("mem"), lax.axis_index("tt")
    y, zh = mem // 4, mem % 4
    x, zl, c = tt // 8, (tt // 2) % 4, tt % 2
    sib = device(x, y, zh, zl, 1 - c)

    def remote(src, dst, ssem, rsem, dev):
        return pltpu.make_async_remote_copy(
            src_ref=src, dst_ref=dst, send_sem=ssem, recv_sem=rsem, device_id=dev, device_id_type=MESH
        )

    load_h = pltpu.make_async_copy(hist, hraw, lsem.at[0])
    load_f = pltpu.make_async_copy(free, fraw, lsem.at[1])
    load_s = pltpu.make_async_copy(start, start_s, lsem.at[2])
    load_n = pltpu.make_async_copy(now, now_s, lsem.at[3])
    load_h.start()
    load_f.start()
    load_s.start()
    load_n.start()

    def z_dev(d):
        z = (zh * 4 + zl + d + 16) % 16
        return device(x, y, z // 4, z % 4, c)

    def x_dev(d):
        return device((x + d) % 4, y, zh, zl, c)

    up, down, far = (y + 1) % 4, (y + 3) % 4, (y + 2) % 4
    up_dev, down_dev = device(x, up, zh, zl, c), device(x, down, zh, zl, c)

    def tell(sem, devs):
        for dev in devs:
            pl.semaphore_signal(sem, inc=1, device_id=dev, device_id_type=MESH)

    barrier = pltpu.get_barrier_semaphore()
    tell(barrier, (up_dev, down_dev, sib, x_dev(1), x_dev(3), z_dev(1), z_dev(-1)))

    load_f.wait()
    for part in range(2):
        for r in range(2):
            rows = pl.ds(pl.multiple_of(y * 64, 64), 64)
            ftmp[part, r] = fraw[part, r, rows, :].astype(F32)
    for part in range(2):
        for r in range(2):
            for t in range(2):
                for ch in range(CHUNKS):
                    at = pl.ds(ch * 2 * ROWS + t, ROWS, stride=2)
                    fpc[t, r, ch, part * ROWS : part * ROWS + ROWS, :] = ftmp[part, r, at, :].astype(BF16)

    load_h.wait()
    for sl in range(4):
        for part in range(2):
            htmp[sl, part] = hraw[part, sl].astype(F32)
        for part in range(2):
            for t in range(2):
                col = (t * 2 + part) * 128
                h_all[y, c, sl * 128 : sl * 128 + 128, col : col + 128] = htmp[
                    sl, part, pl.ds(t, 128, stride=2), :
                ].astype(BF16)

    pl.semaphore_wait(barrier, 7)
    tell(known.at[0], (x_dev(1), x_dev(3), z_dev(1), z_dev(-1)))
    sends = []

    def slab(b, core, sl):
        return h_all.at[b, core, pl.ds(sl * 128, 128), :]

    def hy(b, sl, k, dev):
        cp = remote(slab(b, c, sl), slab(b, c, sl), hy_s.at[k], hy_r.at[k], dev)
        cp.start()
        sends.append(cp)

    def hs(b, sl, k):
        cp = remote(slab(b, c, sl), slab(b, c, sl), hs_s.at[k], hs_r.at[k], sib)
        cp.start()
        sends.append(cp)

    def hy_wait(b, sl, k):
        remote(slab(b, c, sl), slab(b, c, sl), hy_s.at[k], hy_r.at[k], up_dev).wait_recv()

    for k in range(2):
        hy(y, k, k, up_dev)
        hy(y, k + 2, 4 + k, down_dev)
    for k in range(4):
        hs(y, k, k)

    pl.semaphore_wait(known.at[0], 4)
    tell(known.at[1], (z_dev(2), z_dev(-2)))

    @pl.when(c == zh // 2)
    def _():
        fb[...] = fpc[zh % 2, c]
        remote(fpc.at[zh % 2, 1 - c], fb, f_s.at[4], f_r.at[1], sib).start()

    load_s.wait()
    load_n.wait()
    pl.semaphore_wait(known.at[1], 2)
    tell(known.at[2], (z_dev(4), z_dev(-4)))
    tell(known.at[3], (x_dev(1), x_dev(3), x_dev(2)))

    for t in range(2):
        for r in range(2):
            to = 2 * c + t
            mine = (zl == to) & (c == r)

            @pl.when((zl == zh) & mine)
            def _():
                fa[...] = fpc[t, r]

            @pl.when((zl == zh) & jnp.logical_not(mine))
            def _():
                remote(fpc.at[t, r], fa, f_s.at[t * 2 + r], f_r.at[0], device(x, y, zh, to, r)).start()

    for k in range(2):
        hy(y, k + 2, 2 + k, up_dev)
        hy(y, k, 6 + k, down_dev)
    pl.semaphore_wait(known.at[3], 3)
    for k in range(2):
        hy_wait(down, k, k)
        hy(down, k, 8 + k, up_dev)
        hs(down, k, 4 + k)
        hy_wait(up, k + 2, 4 + k)
        hy(up, k + 2, 10 + k, down_dev)
        hs(up, k + 2, 8 + k)

    @pl.when(jnp.logical_not((zl == zh) & (c == zl // 2)))
    def _():
        remote(fpc.at[0, 0], fa, f_s.at[0], f_r.at[0], sib).wait_recv()

    s_time = 16 * x + 4 * zh + zl
    live = jnp.where((start_s[c] <= s_time) & (s_time < now_s[0] + c), 1.0, 0.0).astype(F32)

    def gather(n, ch, value):
        re, im = value[:ROWS].astype(F32), value[ROWS:].astype(F32)
        mod = re * re + im * im
        gsend[n, ch, :ROWS, :] = (-(re * mod) * live).astype(BF16)
        gsend[n, ch, ROWS:, :] = (-(im * mod) * live).astype(BF16)
        for dx, dz in G_ORDER:
            dev = device((x + dx) % 4, y, zh, (zl + dz) % 4, c)
            cp = remote(gsend.at[n, ch], grecv.at[n, ch, x, zl], g_s.at[n, ch, dx * 4 + dz], g_r.at[n, ch, x, zl], dev)
            cp.start()
            sends.append(cp)
        grecv[n, ch, x, zl] = gsend[n, ch]

    def g_wait(n, ch, dx):
        for dz in range(4):
            if dx or dz:
                xs, zs = (x + dx) % 4, (zl + dz) % 4
                b = grecv.at[n, ch, xs, zs]
                remote(b, b, g_s.at[n, ch, 0], g_r.at[n, ch, xs, zs], sib).wait_recv()

    def product(n, ch, b, core):
        left = jnp.concatenate([grecv[n, ch, b, sl] for sl in range(4)], axis=1)
        return jnp.dot(left, h_all[b, core], preferred_element_type=F32)

    def r_blocks(n, ch, acc):
        for t in range(4):
            p = acc[t // 2][:, (t % 2) * 256 : (t % 2) * 256 + 256]
            rsend[n, ch, t, :ROWS, :] = (p[:ROWS, :128] - p[ROWS:, 128:]).astype(BF16)
            rsend[n, ch, t, ROWS:, :] = (p[:ROWS, 128:] + p[ROWS:, :128]).astype(BF16)

    def multiply(n, ch):
        acc = [None, None]
        for d in (0, 1, 3, 2):
            g_wait(n, ch, d)
            for core in range(2):
                prod = product(n, ch, (x + d) % 4, core)
                acc[core] = prod if acc[core] is None else acc[core] + prod
        r_blocks(n, ch, acc)

    def r_here(last, t):
        return (zh == t) if last else (zh == zl) & (zl == t)

    def r_send(n, ch, last):
        for t in range(4):
            dev = device(x, y, t, zl, c) if last else device(x, y, zl, t, c)

            @pl.when(r_here(last, t))
            def _():
                rrecv[n, ch, zh] = rsend[n, ch, t]

            @pl.when(jnp.logical_not(r_here(last, t)))
            def _():
                remote(rsend.at[n, ch, t], rrecv.at[n, ch, zh], r_s.at[n, ch, t], r_r.at[n, ch, zh], dev).start()

    def r_sum(n, ch, last, base):
        for src in range(4):
            here = (zh == src) if last else (zh == zl) & (zh == src)

            @pl.when(jnp.logical_not(here))
            def _():
                b = rrecv.at[n, ch, src]
                remote(b, b, r_s.at[n, ch, src], r_r.at[n, ch, src], sib).wait_recv()

        total = sum(rrecv[n, ch, src].astype(F32) for src in range(4))
        return (base[ch].astype(F32) + COUPLING * total).astype(BF16)

    def flush():
        for cp in sends:
            cp.wait_send()
        sends.clear()

    for ch in range(CHUNKS):
        gather(0, ch, fa[ch])

    for k in range(2):
        hy_wait(down, k + 2, 2 + k)
        hs(down, k + 2, 6 + k)
        hy_wait(up, k, 6 + k)
        hs(up, k, 10 + k)
    pl.semaphore_wait(known.at[2], 2)

    def hs_wait(b, slabs):
        for sl, k in slabs:
            remote(slab(b, 1 - c, sl), slab(b, 1 - c, sl), hs_s.at[k], hs_r.at[k], sib).wait_recv()

    for ch in range(CHUNKS):
        for d in range(4):
            g_wait(0, ch, d)
    hs_wait(y, ((0, 0), (1, 1), (2, 2), (3, 3)))
    hs_wait(down, ((0, 4), (1, 5), (2, 6), (3, 7)))
    hs_wait(up, ((2, 8), (3, 9), (0, 10), (1, 11)))
    own = [sum(product(0, ch, b, c) for b in (y, down, up)) for ch in range(CHUNKS)]
    other = [sum(product(0, ch, b, 1 - c) for b in (y, down, up)) for ch in range(CHUNKS)]
    for k in range(2):
        hy_wait(far, k, 8 + k)
        hs(far, k, 12 + k)
        hy_wait(far, k + 2, 10 + k)
        hs(far, k + 2, 14 + k)
    own = [own[ch] + product(0, ch, far, c) for ch in range(CHUNKS)]
    hs_wait(far, ((0, 12), (1, 13), (2, 14), (3, 15)))

    for n in range(ITERS):
        last = n == ITERS - 1
        for ch in range(CHUNKS):
            if n == 0:
                rest = other[ch] + product(0, ch, far, 1 - c)
                r_blocks(0, ch, [jnp.where(c == 0, own[ch], rest), jnp.where(c == 0, rest, own[ch])])
            else:
                multiply(n, ch)
            r_send(n, ch, last)
        flush()
        if not last:
            for ch in range(CHUNKS):
                gather(n + 1, ch, r_sum(n, ch, last, fa))

    @pl.when(c != zh // 2)
    def _():
        remote(fpc.at[0, 0], fb, f_s.at[4], f_r.at[1], sib).wait_recv()

    core = zh // 2
    for ch in range(CHUNKS):
        xfin[ch] = r_sum(ITERS - 1, ch, True, fb)
        for d in (2, 1, 3, 0):
            dev = device(x, y, (zh + d) % 4, zl, core)

            def go(d=d, dev=dev):
                remote(xfin.at[ch], pieces.at[y, zh % 2, c, ch], az_s.at[ch, d], az_r.at[zh % 2, c, ch], dev).start()

            if d:
                go()
            else:
                @pl.when(core != c)
                def _():
                    go()

                @pl.when(core == c)
                def _():
                    pieces[y, zh % 2, c, ch] = xfin[ch]

    near = jnp.where((zh == 2 * c) | (zh == (2 * c + 3) % 4), 0, 1)
    for order in range(2):
        t = near if order == 0 else 1 - near
        for ch in range(CHUNKS):
            for r in range(2):
                src = pieces.at[y, t, r, ch]

                @pl.when(jnp.logical_not((zh == 2 * c + t) & (c == r)))
                def _():
                    remote(src, src, az_s.at[0, 0], az_r.at[t, r, ch], sib).wait_recv()

                for dy in (2, 1, 3):
                    k = (order * 2 + r) * CHUNKS + ch
                    dev = device(x, (y + dy) % 4, zh, zl, c)
                    cp = remote(src, src, ay_s.at[dy - 1, k], ay_r.at[y, t, r, ch], dev)
                    cp.start()
                    sends.append(cp)

    def assemble(b):
        for t in range(2):
            for r in range(2):
                for part in range(2):
                    for ch in range(CHUNKS):
                        at = pl.ds(pl.multiple_of(b * 64, 64) + ch * 2 * ROWS + t, ROWS, stride=2)
                        otmp[part, r, at, :] = pieces[b, t, r, ch, part * ROWS : part * ROWS + ROWS, :].astype(F32)
        for r in range(2):
            for part in range(2):
                rows = pl.ds(pl.multiple_of(b * 64, 64), 64)
                out[part, r, rows, :] = otmp[part, r, rows, :].astype(BF16)

    assemble(y)
    for dy in (1, 3, 2):
        b = (y + dy) % 4
        for t in range(2):
            for r in range(2):
                for ch in range(CHUNKS):
                    p = pieces.at[b, t, r, ch]
                    remote(p, p, ay_s.at[0, 0], ay_r.at[b, t, r, ch], sib).wait_recv()
        assemble(b)

    for t in range(2):
        for r in range(2):
            @pl.when((zl == zh) & jnp.logical_not((zl == 2 * c + t) & (c == r)))
            def _():
                remote(fpc.at[t, r], fa, f_s.at[t * 2 + r], f_r.at[0], sib).wait_send()

    @pl.when(c == zh // 2)
    def _():
        remote(fpc.at[0, 0], fb, f_s.at[4], f_r.at[1], sib).wait_send()

    for n in range(ITERS):
        for ch in range(CHUNKS):
            for t in range(4):
                @pl.when(jnp.logical_not(r_here(n == ITERS - 1, t)))
                def _():
                    b = rsend.at[n, ch, t]
                    remote(b, b, r_s.at[n, ch, t], r_r.at[n, ch, t], sib).wait_send()
    for ch in range(CHUNKS):
        for d in range(4):
            def done(d=d):
                remote(xfin.at[ch], xfin.at[ch], az_s.at[ch, d], az_r.at[0, 0, ch], sib).wait_send()

            if d:
                done()
            else:
                pl.when(core != c)(done)
    flush()


G_ORDER = tuple(
    sorted(
        ((dx, dz) for dx in range(4) for dz in range(4) if dx or dz),
        key=lambda d: -(min(d[0], 4 - d[0]) + min(d[1], 4 - d[1])),
    )
)


def on_device(history, free_rows, memory_start, now):
    vmem = pltpu.VMEM
    dma = pltpu.SemaphoreType.DMA
    block = (CHUNKS, 2 * ROWS, 128)
    result = pl.pallas_call(
        kernel,
        out_shape=jax.ShapeDtypeStruct((2, 2, 256, 128), BF16),
        in_specs=[pl.BlockSpec(memory_space=pltpu.HBM)] * 4,
        out_specs=pl.BlockSpec(memory_space=pltpu.VMEM),
        scratch_shapes=[
            pltpu.SMEM((2,), jnp.int32),
            pltpu.SMEM((1,), jnp.int32),
            vmem((2, 4, 256, 128), BF16),
            vmem((4, 2, 256, 128), F32),
            vmem((4, 2, 512, 512), BF16),
            vmem((2, 2, 256, 128), BF16),
            vmem((2, 2, 64, 128), F32),
            vmem((2, 2, *block), BF16),
            vmem(block, BF16),
            vmem(block, BF16),
            vmem((ITERS, *block), BF16),
            vmem((ITERS, CHUNKS, 4, 4, *block[1:]), BF16),
            vmem((ITERS, CHUNKS, 4, *block[1:]), BF16),
            vmem((ITERS, CHUNKS, 4, *block[1:]), BF16),
            vmem(block, BF16),
            vmem((4, 2, 2, *block), BF16),
            vmem((2, 2, 256, 128), F32),
            dma((4,)),
            dma((12,)), dma((12,)),
            dma((16,)), dma((16,)),
            dma((5,)), dma((2,)),
            dma((ITERS, CHUNKS, 16)), dma((ITERS, CHUNKS, 4, 4)),
            dma((ITERS, CHUNKS, 4)), dma((ITERS, CHUNKS, 4)),
            dma((CHUNKS, 4)), dma((2, 2, CHUNKS)),
            dma((3, 4 * CHUNKS)), dma((4, 2, 2, CHUNKS)),
            pltpu.SemaphoreType.REGULAR((4,)),
        ],
        compiler_params=pltpu.CompilerParams(
            collective_id=0, has_side_effects=True, vmem_limit_bytes=VMEM_KIB * 1024
        ),
        name="fixed_point",
    )(history.reshape(2, 4, 256, 128), free_rows.reshape(2, 2, 256, 128), memory_start, now)
    return result.reshape(free_rows.shape)


def solution(mesh):
    return jax.shard_map(
        on_device,
        mesh=mesh,
        in_specs=(P(None, "mem", None, "tt", None), P(None, None, None, "tt", None), P(), P()),
        out_specs=P(None, None, None, "tt", None),
        check_vma=False,
    )
```

time: 95 us -> 84.7 us (0.89)
  Pallas kernels: 90.7 us -> 82.6 us
  local copies, waits for them, and re-layouts: 3.34 us -> 1.35 us
    pallas_call x1, Pallas kernels: 90.7 us -> 82.6 us  [on_device(): pl.pallas_call(kernel, out_shape=jax.ShapeDtypeStruct((2, 2, 256, 128), B...]
    unnamed x7 -> x3, local copies, waits for them, and re-layouts: 3.34 us -> 1.35 us
where the time goes in v2:
time: 84.7 us; the launch traced here: 84.6 us
  Pallas kernels  82.6 us (98%)
  local copies, waits for them, and re-layouts  1.35 us (2%)
    pallas_call x1, Pallas kernels, on_device(): pl.pallas_call(kernel, out_shape=jax.ShapeDtypeStruct((2, 2, 256, 128), B...  82.6 us

profile of v2, /device:TPU:1, one launch (start us, length us, event | category | flops | bytes accessed | tf_op | source)
XLA Modules:
  0.0 84.6 jit_solution(8967160307970103582)
XLA Ops:
  0.7 0.0 copy-start
  0.7 0.6 copy-done
  1.3 82.6 %fixed_point.1 = bf16[2,2,256,128]{3,2,1,0:T(8,128)(2,1)S(1)} custom-call(bf16[2,4,256,128]{3,2,1,0:T(8,128)(2,1)} %bitcast.4, bf16[2,2,256,128]{3,2,1,0:T(8,128)(2,1)} %bitcast.5, s32[2]{0:T(128)S(1)} %copy-done, s32[1]{0:T(128)S(6)} %copy.6.now), custom_call_target="tpu_custom_call" | custom-call | tf_op jit(solution)/shard_map/fixed_point/pallas_call | solution.py:379
  83.9 0.7 copy.7
Async XLA Ops:
  0.7 0.7 copy-start

commit v3 on v2

--- a/solution.py
+++ b/solution.py
@@ -23,8 +23,8 @@
 
 def kernel(
     hist, free, start, now, out,
-    start_s, now_s, hraw, htmp, h_all, fraw, ftmp, fpc, fa, fb, gsend, grecv, rsend, rrecv, xfin, pieces, otmp,
-    lsem, hy_s, hy_r, hs_s, hs_r, f_s, f_r, g_s, g_r, r_s, r_r, az_s, az_r, ay_s, ay_r, known,
+    start_s, now_s, hraw, htmp, h_all, fraw, ftmp, fpc, fa, fb, gsend, grecv, gsib, rsend, rrecv, xfin, pieces, otmp,
+    lsem, hy_s, hy_r, hs_s, hs_r, f_s, f_r, g_s, g_r, gs_s, gs_r, r_s, r_r, az_s, az_r, ay_s, ay_r, known,
 ):
     mem, tt = lax.axis_index("mem"), lax.axis_index("tt")
     y, zh = mem // 4, mem % 4
@@ -180,11 +180,9 @@
         left = jnp.concatenate([grecv[n, ch, b, sl] for sl in range(4)], axis=1)
         return jnp.dot(left, h_all[b, core], preferred_element_type=F32)
 
-    def r_blocks(n, ch, acc):
-        for t in range(4):
-            p = acc[t // 2][:, (t % 2) * 256 : (t % 2) * 256 + 256]
-            rsend[n, ch, t, :ROWS, :] = (p[:ROWS, :128] - p[ROWS:, 128:]).astype(BF16)
-            rsend[n, ch, t, ROWS:, :] = (p[:ROWS, 128:] + p[ROWS:, :128]).astype(BF16)
+    def r_block(n, ch, t, p):
+        rsend[n, ch, t, :ROWS, :] = (p[:ROWS, :128] - p[ROWS:, 128:]).astype(BF16)
+        rsend[n, ch, t, ROWS:, :] = (p[:ROWS, 128:] + p[ROWS:, :128]).astype(BF16)
 
     def multiply(n, ch):
         acc = [None, None]
@@ -193,26 +191,43 @@
             for core in range(2):
                 prod = product(n, ch, (x + d) % 4, core)
                 acc[core] = prod if acc[core] is None else acc[core] + prod
-        r_blocks(n, ch, acc)
-
-    def r_here(last, t):
-        return (zh == t) if last else (zh == zl) & (zl == t)
-
-    def r_send(n, ch, last):
         for t in range(4):
-            dev = device(x, y, t, zl, c) if last else device(x, y, zl, t, c)
-
-            @pl.when(r_here(last, t))
+            r_block(n, ch, t, acc[t // 2][:, (t % 2) * 256 : (t % 2) * 256 + 256])
+
+    def r_dest(n, t):
+        if n == ITERS - 1 and n > 0:
+            return device(x, y, t, zl, c)
+        if n > 0:
+            return device(x, y, zl, t, c)
+        return device(x, y, zl, 2 * c + t % 2, c if t < 2 else 1 - c)
+
+    def r_here(n, t):
+        if n == ITERS - 1 and n > 0:
+            return zh == t
+        if n > 0:
+            return (zh == zl) & (zl == t)
+        return (zh == zl) & (zl == 2 * c + t % 2) if t < 2 else False
+
+    def r_send(n, ch):
+        for t in range(4):
+            if r_here(n, t) is not False:
+
+                @pl.when(r_here(n, t))
+                def _():
+                    rrecv[n, ch, zh] = rsend[n, ch, t]
+
+            @pl.when(jnp.logical_not(r_here(n, t)))
             def _():
-                rrecv[n, ch, zh] = rsend[n, ch, t]
-
-            @pl.when(jnp.logical_not(r_here(last, t)))
-            def _():
-                remote(rsend.at[n, ch, t], rrecv.at[n, ch, zh], r_s.at[n, ch, t], r_r.at[n, ch, zh], dev).start()
-
-    def r_sum(n, ch, last, base):
+                remote(rsend.at[n, ch, t], rrecv.at[n, ch, zh], r_s.at[n, ch, t], r_r.at[n, ch, zh], r_dest(n, t)).start()
+
+    def r_sum(n, ch, base):
         for src in range(4):
-            here = (zh == src) if last else (zh == zl) & (zh == src)
+            if n == ITERS - 1 and n > 0:
+                here = zh == src
+            elif n > 0:
+                here = (zh == zl) & (zh == src)
+            else:
+                here = (zh == zl) & (zh == src) & (c == zl // 2)
 
             @pl.when(jnp.logical_not(here))
             def _():
@@ -236,40 +251,53 @@
         hy_wait(up, k, 6 + k)
         hs(up, k, 10 + k)
     pl.semaphore_wait(known.at[2], 2)
-
-    def hs_wait(b, slabs):
+    tell(known.at[4], (sib,))
+
+    for ch in range(CHUNKS):
+        for d in range(4):
+            g_wait(0, ch, d)
+        cp = remote(grecv.at[0, ch], gsib.at[ch], gs_s.at[ch], gs_r.at[ch], sib)
+        cp.start()
+        sends.append(cp)
+    for ch in range(CHUNKS):
+        remote(gsib.at[ch], gsib.at[ch], gs_s.at[ch], gs_r.at[ch], sib).wait_recv()
+
+    def first(b):
+        left = [[jnp.concatenate([g[b, sl] for sl in range(4)], axis=1) for g in (grecv.at[0, ch], gsib.at[ch])]
+                for ch in range(CHUNKS)]
+        return jnp.dot(jnp.concatenate(sum(left, []), axis=0), h_all[b, c], preferred_element_type=F32)
+
+    acc = first(y) + first(down) + first(up)
+    for k in range(2):
+        hy_wait(far, k, 8 + k)
+        hy_wait(far, k + 2, 10 + k)
+    acc = acc + first(far)
+    pl.semaphore_wait(known.at[4], 1)
+    for ch in range(CHUNKS):
+        for t in range(4):
+            at = (ch * 2 + t // 2) * 2 * ROWS
+            r_block(0, ch, t, acc[at : at + 2 * ROWS, (t % 2) * 256 : (t % 2) * 256 + 256])
+        r_send(0, ch)
+    for k in range(2):
+        hs(far, k, 12 + k)
+        hs(far, k + 2, 14 + k)
+    for b, slabs in (
+        (y, ((0, 0), (1, 1), (2, 2), (3, 3))),
+        (down, ((0, 4), (1, 5), (2, 6), (3, 7))),
+        (up, ((2, 8), (3, 9), (0, 10), (1, 11))),
+        (far, ((0, 12), (1, 13), (2, 14), (3, 15))),
+    ):
         for sl, k in slabs:
             remote(slab(b, 1 - c, sl), slab(b, 1 - c, sl), hs_s.at[k], hs_r.at[k], sib).wait_recv()
 
-    for ch in range(CHUNKS):
-        for d in range(4):
-            g_wait(0, ch, d)
-    hs_wait(y, ((0, 0), (1, 1), (2, 2), (3, 3)))
-    hs_wait(down, ((0, 4), (1, 5), (2, 6), (3, 7)))
-    hs_wait(up, ((2, 8), (3, 9), (0, 10), (1, 11)))
-    own = [sum(product(0, ch, b, c) for b in (y, down, up)) for ch in range(CHUNKS)]
-    other = [sum(product(0, ch, b, 1 - c) for b in (y, down, up)) for ch in range(CHUNKS)]
-    for k in range(2):
-        hy_wait(far, k, 8 + k)
-        hs(far, k, 12 + k)
-        hy_wait(far, k + 2, 10 + k)
-        hs(far, k + 2, 14 + k)
-    own = [own[ch] + product(0, ch, far, c) for ch in range(CHUNKS)]
-    hs_wait(far, ((0, 12), (1, 13), (2, 14), (3, 15)))
-
-    for n in range(ITERS):
-        last = n == ITERS - 1
+    for n in range(1, ITERS):
+        flush()
         for ch in range(CHUNKS):
-            if n == 0:
-                rest = other[ch] + product(0, ch, far, 1 - c)
-                r_blocks(0, ch, [jnp.where(c == 0, own[ch], rest), jnp.where(c == 0, rest, own[ch])])
-            else:
-                multiply(n, ch)
-            r_send(n, ch, last)
-        flush()
-        if not last:
-            for ch in range(CHUNKS):
-                gather(n + 1, ch, r_sum(n, ch, last, fa))
+            gather(n, ch, r_sum(n - 1, ch, fa))
+        for ch in range(CHUNKS):
+            multiply(n, ch)
+            r_send(n, ch)
+    flush()
 
     @pl.when(c != zh // 2)
     def _():
@@ -277,7 +305,7 @@
 
     core = zh // 2
     for ch in range(CHUNKS):
-        xfin[ch] = r_sum(ITERS - 1, ch, True, fb)
+        xfin[ch] = r_sum(ITERS - 1, ch, fb)
         for d in (2, 1, 3, 0):
             dev = device(x, y, (zh + d) % 4, zl, core)
 
@@ -348,7 +376,7 @@
     for n in range(ITERS):
         for ch in range(CHUNKS):
             for t in range(4):
-                @pl.when(jnp.logical_not(r_here(n == ITERS - 1, t)))
+                @pl.when(jnp.logical_not(r_here(n, t)))
                 def _():
                     b = rsend.at[n, ch, t]
                     remote(b, b, r_s.at[n, ch, t], r_r.at[n, ch, t], sib).wait_send()
@@ -394,6 +422,7 @@
             vmem(block, BF16),
             vmem((ITERS, *block), BF16),
             vmem((ITERS, CHUNKS, 4, 4, *block[1:]), BF16),
+            vmem((CHUNKS, 4, 4, *block[1:]), BF16),
             vmem((ITERS, CHUNKS, 4, *block[1:]), BF16),
             vmem((ITERS, CHUNKS, 4, *block[1:]), BF16),
             vmem(block, BF16),
@@ -404,10 +433,11 @@
             dma((16,)), dma((16,)),
             dma((5,)), dma((2,)),
             dma((ITERS, CHUNKS, 16)), dma((ITERS, CHUNKS, 4, 4)),
+            dma((CHUNKS,)), dma((CHUNKS,)),
             dma((ITERS, CHUNKS, 4)), dma((ITERS, CHUNKS, 4)),
             dma((CHUNKS, 4)), dma((2, 2, CHUNKS)),
             dma((3, 4 * CHUNKS)), dma((4, 2, 2, CHUNKS)),
-            pltpu.SemaphoreType.REGULAR((4,)),
+            pltpu.SemaphoreType.REGULAR((5,)),
         ],
         compiler_params=pltpu.CompilerParams(
             collective_id=0, has_side_effects=True, vmem_limit_bytes=VMEM_KIB * 1024

time: 84.7 us -> 82.7 us (0.976)
  Pallas kernels: 82.6 us -> 80.5 us
    pallas_call x1, Pallas kernels: 82.6 us -> 80.5 us  [on_device(): pl.pallas_call(kernel, out_shape=jax.ShapeDtypeStruct((2, 2, 256, 128), B...]
where the time goes in v3:
time: 82.7 us; the launch traced here: 82.5 us
  Pallas kernels  80.5 us (97%)
  local copies, waits for them, and re-layouts  1.35 us (2%)
    pallas_call x1, Pallas kernels, on_device(): pl.pallas_call(kernel, out_shape=jax.ShapeDtypeStruct((2, 2, 256, 128), B...  80.5 us

profile of v3, /device:TPU:1, one launch (start us, length us, event | category | flops | bytes accessed | tf_op | source)
XLA Modules:
  0.0 82.5 jit_solution(13210832301300872009)
XLA Ops:
  0.7 0.0 copy-start
  0.7 0.6 copy-done
  1.3 80.5 %fixed_point.1 = bf16[2,2,256,128]{3,2,1,0:T(8,128)(2,1)S(1)} custom-call(bf16[2,4,256,128]{3,2,1,0:T(8,128)(2,1)} %bitcast.4, bf16[2,2,256,128]{3,2,1,0:T(8,128)(2,1)} %bitcast.5, s32[2]{0:T(128)S(1)} %copy-done, s32[1]{0:T(128)S(6)} %copy.6.now), custom_call_target="tpu_custom_call" | custom-call | tf_op jit(solution)/shard_map/fixed_point/pallas_call | solution.py:407
  81.8 0.7 copy.7
Async XLA Ops:
  0.7 0.7 copy-start

commit v4 on v3

--- a/solution.py
+++ b/solution.py
@@ -13,7 +13,7 @@
 BF16 = jnp.bfloat16
 F32 = jnp.float32
 CHUNKS = 2
-VMEM_KIB = 54784
+VMEM_KIB = 48 * 1024
 ROWS = 32 // CHUNKS
 
 
@@ -45,9 +45,9 @@
     load_s.start()
     load_n.start()
 
-    def z_dev(d):
+    def z_dev(d, core=c):
         z = (zh * 4 + zl + d + 16) % 16
-        return device(x, y, z // 4, z % 4, c)
+        return device(x, y, z // 4, z % 4, core)
 
     def x_dev(d):
         return device((x + d) % 4, y, zh, zl, c)
@@ -114,11 +114,6 @@
     pl.semaphore_wait(known.at[0], 4)
     tell(known.at[1], (z_dev(2), z_dev(-2)))
 
-    @pl.when(c == zh // 2)
-    def _():
-        fb[...] = fpc[zh % 2, c]
-        remote(fpc.at[zh % 2, 1 - c], fb, f_s.at[4], f_r.at[1], sib).start()
-
     load_s.wait()
     load_n.wait()
     pl.semaphore_wait(known.at[1], 2)
@@ -137,6 +132,11 @@
             @pl.when((zl == zh) & jnp.logical_not(mine))
             def _():
                 remote(fpc.at[t, r], fa, f_s.at[t * 2 + r], f_r.at[0], device(x, y, zh, to, r)).start()
+
+    @pl.when(c == zh // 2)
+    def _():
+        for r in range(2):
+            remote(fpc.at[zh % 2, r], fb, f_s.at[4 + r], f_r.at[1], z_dev(2, r)).start()
 
     for k in range(2):
         hy(y, k + 2, 2 + k, up_dev)
@@ -196,14 +196,14 @@
 
     def r_dest(n, t):
         if n == ITERS - 1 and n > 0:
-            return device(x, y, t, zl, c)
+            return z_dev(2 + 4 * (t - zh) + 16)
         if n > 0:
             return device(x, y, zl, t, c)
         return device(x, y, zl, 2 * c + t % 2, c if t < 2 else 1 - c)
 
     def r_here(n, t):
         if n == ITERS - 1 and n > 0:
-            return zh == t
+            return False
         if n > 0:
             return (zh == zl) & (zl == t)
         return (zh == zl) & (zl == 2 * c + t % 2) if t < 2 else False
@@ -223,7 +223,7 @@
     def r_sum(n, ch, base):
         for src in range(4):
             if n == ITERS - 1 and n > 0:
-                here = zh == src
+                here = False
             elif n > 0:
                 here = (zh == zl) & (zh == src)
             else:
@@ -299,41 +299,25 @@
             r_send(n, ch)
     flush()
 
-    @pl.when(c != zh // 2)
-    def _():
-        remote(fpc.at[0, 0], fb, f_s.at[4], f_r.at[1], sib).wait_recv()
-
-    core = zh // 2
+    remote(fpc.at[0, 0], fb, f_s.at[4], f_r.at[1], sib).wait_recv()
+
+    block = (zh + 3 + zl // 2) % 4
     for ch in range(CHUNKS):
         xfin[ch] = r_sum(ITERS - 1, ch, fb)
-        for d in (2, 1, 3, 0):
-            dev = device(x, y, (zh + d) % 4, zl, core)
-
-            def go(d=d, dev=dev):
-                remote(xfin.at[ch], pieces.at[y, zh % 2, c, ch], az_s.at[ch, d], az_r.at[zh % 2, c, ch], dev).start()
-
-            if d:
-                go()
-            else:
-                @pl.when(core != c)
-                def _():
-                    go()
-
-                @pl.when(core == c)
-                def _():
-                    pieces[y, zh % 2, c, ch] = xfin[ch]
-
-    near = jnp.where((zh == 2 * c) | (zh == (2 * c + 3) % 4), 0, 1)
+        for k, d in enumerate((6, -6, 2, -2)):
+            remote(
+                xfin.at[ch], pieces.at[y, block % 2, c, ch], az_s.at[ch, k], az_r.at[block % 2, c, ch],
+                z_dev(d, block // 2),
+            ).start()
+
+    near = jnp.where((2 * c - zh + 4) % 4 == 2, 1, 0)
     for order in range(2):
         t = near if order == 0 else 1 - near
         for ch in range(CHUNKS):
             for r in range(2):
                 src = pieces.at[y, t, r, ch]
 
-                @pl.when(jnp.logical_not((zh == 2 * c + t) & (c == r)))
-                def _():
-                    remote(src, src, az_s.at[0, 0], az_r.at[t, r, ch], sib).wait_recv()
-
+                remote(src, src, az_s.at[0, 0], az_r.at[t, r, ch], sib).wait_recv()
                 for dy in (2, 1, 3):
                     k = (order * 2 + r) * CHUNKS + ch
                     dev = device(x, (y + dy) % 4, zh, zl, c)
@@ -371,7 +355,8 @@
 
     @pl.when(c == zh // 2)
     def _():
-        remote(fpc.at[0, 0], fb, f_s.at[4], f_r.at[1], sib).wait_send()
+        for r in range(2):
+            remote(fpc.at[0, 0], fb, f_s.at[4 + r], f_r.at[1], sib).wait_send()
 
     for n in range(ITERS):
         for ch in range(CHUNKS):
@@ -381,14 +366,8 @@
                     b = rsend.at[n, ch, t]
                     remote(b, b, r_s.at[n, ch, t], r_r.at[n, ch, t], sib).wait_send()
     for ch in range(CHUNKS):
-        for d in range(4):
-            def done(d=d):
-                remote(xfin.at[ch], xfin.at[ch], az_s.at[ch, d], az_r.at[0, 0, ch], sib).wait_send()
-
-            if d:
-                done()
-            else:
-                pl.when(core != c)(done)
+        for k in range(4):
+            remote(xfin.at[ch], xfin.at[ch], az_s.at[ch, k], az_r.at[0, 0, ch], sib).wait_send()
     flush()
 
 
@@ -431,7 +410,7 @@
             dma((4,)),
             dma((12,)), dma((12,)),
             dma((16,)), dma((16,)),
-            dma((5,)), dma((2,)),
+            dma((6,)), dma((2,)),
             dma((ITERS, CHUNKS, 16)), dma((ITERS, CHUNKS, 4, 4)),
             dma((CHUNKS,)), dma((CHUNKS,)),
             dma((ITERS, CHUNKS, 4)), dma((ITERS, CHUNKS, 4)),
@@ -443,7 +422,13 @@
             collective_id=0, has_side_effects=True, vmem_limit_bytes=VMEM_KIB * 1024
         ),
         name="fixed_point",
-    )(history.reshape(2, 4, 256, 128), free_rows.reshape(2, 2, 256, 128), memory_start, now)
+    )(
+        *(
+            pltpu.with_memory_space_constraint(array, pltpu.HBM)
+            for array in (history.reshape(2, 4, 256, 128), free_rows.reshape(2, 2, 256, 128), memory_start)
+        ),
+        now,
+    )
     return result.reshape(free_rows.shape)
 
 

time: 82.7 us -> 81.9 us (level)
  no operation moved by 1% of the time
where the time goes in v4:
time: 81.9 us; the launch traced here: 81.7 us
  Pallas kernels  80.4 us (98%)
    pallas_call x1, Pallas kernels, on_device(): pl.pallas_call(kernel, out_shape=jax.ShapeDtypeStruct((2, 2, 256, 128), B...  80.4 us

profile of v4, /device:TPU:1, one launch (start us, length us, event | category | flops | bytes accessed | tf_op | source)
XLA Modules:
  0.0 81.7 jit_solution(428863696510058987)
XLA Ops:
  0.7 80.4 %fixed_point.1 = bf16[2,2,256,128]{3,2,1,0:T(8,128)(2,1)S(1)} custom-call(bf16[2,4,256,128]{3,2,1,0:T(8,128)(2,1)} %bitcast.4, bf16[2,2,256,128]{3,2,1,0:T(8,128)(2,1)} %bitcast.5, s32[2]{0:T(128)} %start.1, s32[1]{0:T(128)S(6)} %copy.6.now), custom_call_target="tpu_custom_call" | custom-call | tf_op jit(solution)/shard_map/fixed_point/pallas_call | solution.py:386
  81.0 0.7 copy.7

commit v5 on v4

--- a/solution.py
+++ b/solution.py
@@ -87,7 +87,8 @@
 
     pl.semaphore_wait(barrier, 7)
     tell(known.at[0], (x_dev(1), x_dev(3), z_dev(1), z_dev(-1)))
-    sends = []
+    sends, gathers = [], []
+    fifteen = h_all.at[0, 0, pl.ds(0, 15 * 2 * ROWS), pl.ds(0, 128)]
 
     def slab(b, core, sl):
         return h_all.at[b, core, pl.ds(sl * 128, 128), :]
@@ -164,17 +165,13 @@
         gsend[n, ch, ROWS:, :] = (-(im * mod) * live).astype(BF16)
         for dx, dz in G_ORDER:
             dev = device((x + dx) % 4, y, zh, (zl + dz) % 4, c)
-            cp = remote(gsend.at[n, ch], grecv.at[n, ch, x, zl], g_s.at[n, ch, dx * 4 + dz], g_r.at[n, ch, x, zl], dev)
-            cp.start()
-            sends.append(cp)
+            remote(gsend.at[n, ch], grecv.at[n, ch, x, zl], g_s.at[n, ch], g_r.at[n, ch, (4 - dx) % 4], dev).start()
+        gathers.append((n, ch))
         grecv[n, ch, x, zl] = gsend[n, ch]
 
     def g_wait(n, ch, dx):
-        for dz in range(4):
-            if dx or dz:
-                xs, zs = (x + dx) % 4, (zl + dz) % 4
-                b = grecv.at[n, ch, xs, zs]
-                remote(b, b, g_s.at[n, ch, 0], g_r.at[n, ch, xs, zs], sib).wait_recv()
+        b = grecv.at[n, ch, (x + dx) % 4, pl.ds(0, 4 if dx else 3)]
+        remote(b, b, g_s.at[n, ch], g_r.at[n, ch, dx], sib).wait_recv()
 
     def product(n, ch, b, core):
         left = jnp.concatenate([grecv[n, ch, b, sl] for sl in range(4)], axis=1)
@@ -241,6 +238,10 @@
         for cp in sends:
             cp.wait_send()
         sends.clear()
+        for n, ch in gathers:
+            b = fifteen
+            remote(b, b, g_s.at[n, ch], g_r.at[n, ch, 0], sib).wait_send()
+        gathers.clear()
 
     for ch in range(CHUNKS):
         gather(0, ch, fa[ch])
@@ -319,11 +320,8 @@
 
                 remote(src, src, az_s.at[0, 0], az_r.at[t, r, ch], sib).wait_recv()
                 for dy in (2, 1, 3):
-                    k = (order * 2 + r) * CHUNKS + ch
                     dev = device(x, (y + dy) % 4, zh, zl, c)
-                    cp = remote(src, src, ay_s.at[dy - 1, k], ay_r.at[y, t, r, ch], dev)
-                    cp.start()
-                    sends.append(cp)
+                    remote(src, src, ay_s.at[dy - 1], ay_r.at[y], dev).start()
 
     def assemble(b):
         for t in range(2):
@@ -340,11 +338,7 @@
     assemble(y)
     for dy in (1, 3, 2):
         b = (y + dy) % 4
-        for t in range(2):
-            for r in range(2):
-                for ch in range(CHUNKS):
-                    p = pieces.at[b, t, r, ch]
-                    remote(p, p, ay_s.at[0, 0], ay_r.at[b, t, r, ch], sib).wait_recv()
+        remote(pieces.at[b], pieces.at[b], ay_s.at[0], ay_r.at[b], sib).wait_recv()
         assemble(b)
 
     for t in range(2):
@@ -369,6 +363,8 @@
         for k in range(4):
             remote(xfin.at[ch], xfin.at[ch], az_s.at[ch, k], az_r.at[0, 0, ch], sib).wait_send()
     flush()
+    for dy in range(1, 4):
+        remote(pieces.at[0], pieces.at[0], ay_s.at[dy - 1], ay_r.at[0], sib).wait_send()
 
 
 G_ORDER = tuple(
@@ -411,11 +407,11 @@
             dma((12,)), dma((12,)),
             dma((16,)), dma((16,)),
             dma((6,)), dma((2,)),
-            dma((ITERS, CHUNKS, 16)), dma((ITERS, CHUNKS, 4, 4)),
+            dma((ITERS, CHUNKS)), dma((ITERS, CHUNKS, 4)),
             dma((CHUNKS,)), dma((CHUNKS,)),
             dma((ITERS, CHUNKS, 4)), dma((ITERS, CHUNKS, 4)),
             dma((CHUNKS, 4)), dma((2, 2, CHUNKS)),
-            dma((3, 4 * CHUNKS)), dma((4, 2, 2, CHUNKS)),
+            dma((3,)), dma((4,)),
             pltpu.SemaphoreType.REGULAR((5,)),
         ],
         compiler_params=pltpu.CompilerParams(

time: 81.9 us -> 80.1 us (0.978)
  Pallas kernels: 80.4 us -> 78.6 us
    pallas_call x1, Pallas kernels: 80.4 us -> 78.6 us  [on_device(): pl.pallas_call(kernel, out_shape=jax.ShapeDtypeStruct((2, 2, 256, 128), B...]
where the time goes in v5:
time: 80.1 us; the launch traced here: 80 us
  Pallas kernels  78.6 us (98%)
    pallas_call x1, Pallas kernels, on_device(): pl.pallas_call(kernel, out_shape=jax.ShapeDtypeStruct((2, 2, 256, 128), B...  78.6 us

profile of v5, /device:TPU:1, one launch (start us, length us, event | category | flops | bytes accessed | tf_op | source)
XLA Modules:
  0.0 80.0 jit_solution(17629316533922356820)
XLA Ops:
  0.7 78.6 %fixed_point.1 = bf16[2,2,256,128]{3,2,1,0:T(8,128)(2,1)S(1)} custom-call(bf16[2,4,256,128]{3,2,1,0:T(8,128)(2,1)} %bitcast.4, bf16[2,2,256,128]{3,2,1,0:T(8,128)(2,1)} %bitcast.5, s32[2]{0:T(128)} %start.1, s32[1]{0:T(128)S(6)} %copy.6.now), custom_call_target="tpu_custom_call" | custom-call | tf_op jit(solution)/shard_map/fixed_point/pallas_call | solution.py:382
  79.3 0.7 copy.7

commit v6 on v5

--- a/solution.py
+++ b/solution.py
@@ -215,21 +215,23 @@
 
             @pl.when(jnp.logical_not(r_here(n, t)))
             def _():
-                remote(rsend.at[n, ch, t], rrecv.at[n, ch, zh], r_s.at[n, ch, t], r_r.at[n, ch, zh], r_dest(n, t)).start()
+                remote(rsend.at[n, ch, t], rrecv.at[n, ch, zh], r_s.at[n, ch, t], r_r.at[n, ch], r_dest(n, t)).start()
 
     def r_sum(n, ch, base):
-        for src in range(4):
-            if n == ITERS - 1 and n > 0:
-                here = False
-            elif n > 0:
-                here = (zh == zl) & (zh == src)
-            else:
-                here = (zh == zl) & (zh == src) & (c == zl // 2)
+        b = rrecv.at[n, ch]
+        if n == ITERS - 1 and n > 0:
+            remote(b, b, r_s.at[n, ch, 0], r_r.at[n, ch], sib).wait_recv()
+        else:
+            here = (zh == zl) if n > 0 else (zh == zl) & (c == zl // 2)
+
+            @pl.when(here)
+            def _():
+                three = rrecv.at[n, ch, pl.ds(0, 3)]
+                remote(three, three, r_s.at[n, ch, 0], r_r.at[n, ch], sib).wait_recv()
 
             @pl.when(jnp.logical_not(here))
             def _():
-                b = rrecv.at[n, ch, src]
-                remote(b, b, r_s.at[n, ch, src], r_r.at[n, ch, src], sib).wait_recv()
+                remote(b, b, r_s.at[n, ch, 0], r_r.at[n, ch], sib).wait_recv()
 
         total = sum(rrecv[n, ch, src].astype(F32) for src in range(4))
         return (base[ch].astype(F32) + COUPLING * total).astype(BF16)
@@ -307,21 +309,38 @@
         xfin[ch] = r_sum(ITERS - 1, ch, fb)
         for k, d in enumerate((6, -6, 2, -2)):
             remote(
-                xfin.at[ch], pieces.at[y, block % 2, c, ch], az_s.at[ch, k], az_r.at[block % 2, c, ch],
+                xfin.at[ch], pieces.at[y, block % 2, ch, c], az_s.at[ch, k], az_r.at[block % 2, ch],
                 z_dev(d, block // 2),
             ).start()
+
+    for t in range(2):
+        for r in range(2):
+            @pl.when((zl == zh) & jnp.logical_not((zl == 2 * c + t) & (c == r)))
+            def _():
+                remote(fpc.at[t, r], fa, f_s.at[t * 2 + r], f_r.at[0], sib).wait_send()
+
+    @pl.when(c == zh // 2)
+    def _():
+        for r in range(2):
+            remote(fpc.at[0, 0], fb, f_s.at[4 + r], f_r.at[1], sib).wait_send()
+
+    for n in range(ITERS):
+        for ch in range(CHUNKS):
+            for t in range(4):
+                @pl.when(jnp.logical_not(r_here(n, t)))
+                def _():
+                    b = rsend.at[n, ch, t]
+                    remote(b, b, r_s.at[n, ch, t], r_r.at[n, ch], sib).wait_send()
 
     near = jnp.where((2 * c - zh + 4) % 4 == 2, 1, 0)
     for order in range(2):
         t = near if order == 0 else 1 - near
         for ch in range(CHUNKS):
-            for r in range(2):
-                src = pieces.at[y, t, r, ch]
-
-                remote(src, src, az_s.at[0, 0], az_r.at[t, r, ch], sib).wait_recv()
-                for dy in (2, 1, 3):
-                    dev = device(x, (y + dy) % 4, zh, zl, c)
-                    remote(src, src, ay_s.at[dy - 1], ay_r.at[y], dev).start()
+            src = pieces.at[y, t, ch]
+            remote(src, src, az_s.at[0, 0], az_r.at[t, ch], sib).wait_recv()
+            for dy in (2, 1, 3):
+                dev = device(x, (y + dy) % 4, zh, zl, c)
+                remote(src, src, ay_s.at[dy - 1], ay_r.at[y], dev).start()
 
     def assemble(b):
         for t in range(2):
@@ -329,7 +348,7 @@
                 for part in range(2):
                     for ch in range(CHUNKS):
                         at = pl.ds(pl.multiple_of(b * 64, 64) + ch * 2 * ROWS + t, ROWS, stride=2)
-                        otmp[part, r, at, :] = pieces[b, t, r, ch, part * ROWS : part * ROWS + ROWS, :].astype(F32)
+                        otmp[part, r, at, :] = pieces[b, t, ch, r, part * ROWS : part * ROWS + ROWS, :].astype(F32)
         for r in range(2):
             for part in range(2):
                 rows = pl.ds(pl.multiple_of(b * 64, 64), 64)
@@ -341,27 +360,9 @@
         remote(pieces.at[b], pieces.at[b], ay_s.at[0], ay_r.at[b], sib).wait_recv()
         assemble(b)
 
-    for t in range(2):
-        for r in range(2):
-            @pl.when((zl == zh) & jnp.logical_not((zl == 2 * c + t) & (c == r)))
-            def _():
-                remote(fpc.at[t, r], fa, f_s.at[t * 2 + r], f_r.at[0], sib).wait_send()
-
-    @pl.when(c == zh // 2)
-    def _():
-        for r in range(2):
-            remote(fpc.at[0, 0], fb, f_s.at[4 + r], f_r.at[1], sib).wait_send()
-
-    for n in range(ITERS):
-        for ch in range(CHUNKS):
-            for t in range(4):
-                @pl.when(jnp.logical_not(r_here(n, t)))
-                def _():
-                    b = rsend.at[n, ch, t]
-                    remote(b, b, r_s.at[n, ch, t], r_r.at[n, ch, t], sib).wait_send()
     for ch in range(CHUNKS):
         for k in range(4):
-            remote(xfin.at[ch], xfin.at[ch], az_s.at[ch, k], az_r.at[0, 0, ch], sib).wait_send()
+            remote(xfin.at[ch], xfin.at[ch], az_s.at[ch, k], az_r.at[0, ch], sib).wait_send()
     flush()
     for dy in range(1, 4):
         remote(pieces.at[0], pieces.at[0], ay_s.at[dy - 1], ay_r.at[0], sib).wait_send()
@@ -401,7 +402,7 @@
             vmem((ITERS, CHUNKS, 4, *block[1:]), BF16),
             vmem((ITERS, CHUNKS, 4, *block[1:]), BF16),
             vmem(block, BF16),
-            vmem((4, 2, 2, *block), BF16),
+            vmem((4, 2, CHUNKS, 2, *block[1:]), BF16),
             vmem((2, 2, 256, 128), F32),
             dma((4,)),
             dma((12,)), dma((12,)),
@@ -409,8 +410,8 @@
             dma((6,)), dma((2,)),
             dma((ITERS, CHUNKS)), dma((ITERS, CHUNKS, 4)),
             dma((CHUNKS,)), dma((CHUNKS,)),
-            dma((ITERS, CHUNKS, 4)), dma((ITERS, CHUNKS, 4)),
-            dma((CHUNKS, 4)), dma((2, 2, CHUNKS)),
+            dma((ITERS, CHUNKS, 4)), dma((ITERS, CHUNKS)),
+            dma((CHUNKS, 4)), dma((2, CHUNKS)),
             dma((3,)), dma((4,)),
             pltpu.SemaphoreType.REGULAR((5,)),
         ],

time: 80.1 us -> 79.8 us (level)
  no operation moved by 1% of the time
where the time goes in v6:
time: 79.8 us; the launch traced here: 79.7 us
  Pallas kernels  78.3 us (98%)
    pallas_call x1, Pallas kernels, on_device(): pl.pallas_call(kernel, out_shape=jax.ShapeDtypeStruct((2, 2, 256, 128), B...  78.3 us

profile of v6, /device:TPU:1, one launch (start us, length us, event | category | flops | bytes accessed | tf_op | source)
XLA Modules:
  0.0 79.7 jit_solution(5970985523307913370)
XLA Ops:
  0.7 78.3 %fixed_point.1 = bf16[2,2,256,128]{3,2,1,0:T(8,128)(2,1)S(1)} custom-call(bf16[2,4,256,128]{3,2,1,0:T(8,128)(2,1)} %bitcast.4, bf16[2,2,256,128]{3,2,1,0:T(8,128)(2,1)} %bitcast.5, s32[2]{0:T(128)} %start.1, s32[1]{0:T(128)S(6)} %copy.6.now), custom_call_target="tpu_custom_call" | custom-call | tf_op jit(solution)/shard_map/fixed_point/pallas_call | solution.py:383
  79.0 0.7 copy.7
